TPU v7x, 32 devices: a whole 2x2x4 slice. The times are simulated.
32 devices in a mesh: grp: 2 (over x), dp: 16 (over z, y, core).
Axes of the slice: x: 2, y: 2, z: 4, core: 2. Of those that a mesh axis runs over, the one named last changes fastest.
Arguments:
- start_state: bfloat16 [4096, 512], P(('grp', 'dp')), may hold values from -6 to 6
- w_up: bfloat16 [512, 1024], replicated, may hold values from -0.25 to 0.25
- b_up: float32 [1024], replicated, may hold values from -3 to 3
- w_down: bfloat16 [1024, 512], replicated, may hold values from -0.1875 to 0.1875
- w_spread: bfloat16 [512, 1024], replicated, may hold values from -0.25 to 0.25
- w_scale: bfloat16 [1024, 512], replicated, may hold values from -0.1875 to 0.1875
- b_scale: float32 [512], replicated, may hold values from -4 to 4
- brownian_noise: bfloat16 [3, 4096, 512], P(None, ('grp', 'dp')), may hold values from -5 to 5
- step_mults: int32 [3, 4096], P(None, ('grp', 'dp')), may hold values from 1 to 4
- accept_flags: int32 [3, 4096], P(None, ('grp', 'dp')), may hold values 0 or 1
- cotangent: bfloat16 [4096, 512], P(('grp', 'dp')), may hold values from -6 to 6
Outputs:
- err_norms: float32 [3], replicated
- grad_up: float32 [512, 1024], P('dp')
- grad_down: float32 [512, 1024], P('dp')
All inputs are finite; a program needn't handle non-finite values. No bound on the sum of `accept_flags` on one device may be relied on, other than what follows from the above.
Results may differ from a plain program's by a relative error of at most 0.0033.
Values sent between devices are 32-bit elements; how exact they have to be, the bound alone decides.
A program may use at most 64 MiB of HBM per device.

v0:
```python
import jax
import jax.numpy as jnp
from jax import lax
from jax.sharding import PartitionSpec as P

base_step = 0.05
abs_tol = 0.01
rel_tol = 0.01


def diffuse(current, w_first, w_second, b_second):
    inner = jax.nn.silu(
        jnp.dot(current.astype(jnp.bfloat16), w_first, preferred_element_type=jnp.float32)
    )
    outer = jnp.dot(inner.astype(jnp.bfloat16), w_second, preferred_element_type=jnp.float32)
    return 0.6 * jax.nn.sigmoid(outer + b_second)


def forward_step(
    current, w_up, b_up, w_down, w_spread, w_scale, b_scale, noise_now, mult_now, flag_now
):
    low_state = current.astype(jnp.bfloat16)
    pre_act = jnp.dot(low_state, w_up, preferred_element_type=jnp.float32) + b_up
    hidden = jax.nn.silu(pre_act).astype(jnp.bfloat16)
    drift_out = jnp.dot(hidden, w_down, preferred_element_type=jnp.float32)
    step_size = mult_now.astype(jnp.float32)[:, None] * base_step
    sqrt_step = jnp.sqrt(step_size)
    brownian = sqrt_step * noise_now.astype(jnp.float32)
    keep_mask = flag_now.astype(jnp.float32)[:, None]

    def update(before):
        spread = diffuse(before, w_spread, w_scale, b_scale)
        shifted = diffuse(before + spread * sqrt_step, w_spread, w_scale, b_scale)
        milstein = (shifted - spread) * (brownian * brownian - step_size) / (2.0 * sqrt_step)
        proposal = before + drift_out * step_size + spread * brownian + milstein
        return (keep_mask * proposal + (1.0 - keep_mask) * before, milstein)

    (advanced, milstein), pull_back = jax.vjp(update, current)
    scaled = milstein / (abs_tol + rel_tol * jnp.abs(current))
    err_part = jnp.sum(scaled * scaled)
    return (advanced, err_part, (low_state, pre_act, hidden, pull_back, step_size, keep_mask))


def backward_step(cot_state, record, w_up, w_down, grad_up, grad_down):
    low_state, pre_act, hidden, pull_back, step_size, keep_mask = record
    cot_drift = (cot_state * keep_mask * step_size).astype(jnp.bfloat16)
    grad_down = grad_down + lax.dot_general(
        cot_drift, hidden, (((0,), (0,)), ((), ())), preferred_element_type=jnp.float32
    )
    sigma = jax.nn.sigmoid(pre_act)
    back_pre = lax.dot_general(
        cot_drift, w_down, (((1,), (1,)), ((), ())), preferred_element_type=jnp.float32
    )
    cot_pre = (back_pre * sigma * (1.0 + pre_act * (1.0 - sigma))).astype(jnp.bfloat16)
    grad_up = grad_up + lax.dot_general(
        low_state, cot_pre, (((0,), (0,)), ((), ())), preferred_element_type=jnp.float32
    )
    through = pull_back((cot_state, jnp.zeros_like(cot_state)))[0]
    cot_state = through + lax.dot_general(
        cot_pre, w_up, (((1,), (1,)), ((), ())), preferred_element_type=jnp.float32
    )
    return (cot_state, grad_up, grad_down)


def per_device(
    start_state,
    w_up,
    b_up,
    w_down,
    w_spread,
    w_scale,
    b_scale,
    brownian_noise,
    step_mults,
    accept_flags,
    cotangent,
):
    groups = lax.axis_size("grp")
    members = lax.axis_size("dp")
    row_count = start_state.shape[0] * start_state.shape[1] * groups * members
    step_count = brownian_noise.shape[0]
    current = start_state.astype(jnp.float32)
    records = []
    err_sums = []
    for step_index in range(step_count):
        current, err_part, record = forward_step(
            current,
            w_up,
            b_up,
            w_down,
            w_spread,
            w_scale,
            b_scale,
            brownian_noise[step_index],
            step_mults[step_index],
            accept_flags[step_index],
        )
        records.append(record)
        err_sums.append(err_part)
    totals = lax.psum(jnp.stack(err_sums), ("grp", "dp"))
    err_norms = jnp.sqrt(totals / row_count)
    cot_state = cotangent.astype(jnp.float32)
    grad_up = jnp.zeros(w_up.shape, jnp.float32)
    grad_down = jnp.zeros((w_down.shape[1], w_down.shape[0]), jnp.float32)
    for step_index in reversed(range(step_count)):
        cot_state, grad_up, grad_down = backward_step(
            cot_state, records[step_index], w_up, w_down, grad_up, grad_down
        )
    inner_up, inner_down = (
        lax.psum_scatter(grad_up, "dp", scatter_dimension=0, tiled=True),
        lax.psum_scatter(grad_down, "dp", scatter_dimension=0, tiled=True),
    )
    grad_up, grad_down = lax.psum((inner_up, inner_down), "grp")
    return (err_norms, grad_up, grad_down)


def solution(mesh):
    in_specs = (
        P(("grp", "dp"), None),
        P(),
        P(),
        P(),
        P(),
        P(),
        P(),
        P(None, ("grp", "dp"), None),
        P(None, ("grp", "dp")),
        P(None, ("grp", "dp")),
        P(("grp", "dp"), None),
    )
    out_specs = (P(), P("dp", None), P("dp", None))
    return jax.shard_map(
        per_device, mesh=mesh, in_specs=in_specs, out_specs=out_specs, check_vma=False
    )
```

profile of v0, /device:TPU:0, one launch (start us, length us, event | category | flops | bytes accessed | tf_op | source)
XLA Modules:
  0.0 234.4 jit_solution(15339135114082320699)
XLA Ops:
  8.0 1.3 broadcast_subtract_fusion
  11.0 1.5 convolution_add_fusion.2
  12.6 2.0 fusion.48
  14.7 2.0 fusion.151
  16.7 1.8 fusion.37
  25.0 1.9 multiply_reduce_fusion
  27.4 3.2 %fusion.55 = f32[128,512]{1,0:T(8,128)} fusion(bf16[512,1024]{1,0:T(8,128)(2,1)S(1)} %copy-done, f32[128,1024]{1,0:T(8,128)} %copy-done.17, bf16[1024,512]{1,0:T(8,128)(2,1)} %param.16, f32[128,512]{1,0:T(8,128)} %get-tuple-element.26, bf16[128,512]{1,0:T(8,128)(2,1)S(1)} %copy-done.19, f32[128]{0:T(128)S(1)} %get-tuple-element.16, f32[128]{0:T(128)} %copy-done.33, ...), kind=kOutput, calls=%fused_computation.81 | convolution fusion | flops 270794752 | bytes 3409920 | tf_op jit(solution)/shard_map/transpose(jvp())/dot_general | solution.py:13
  30.6 3.2 %fusion.54 = f32[128,512]{1,0:T(8,128)} fusion(bf16[512,1024]{1,0:T(8,128)(2,1)S(1)} %copy-done, f32[128,1024]{1,0:T(8,128)} %copy-done.16, bf16[1024,512]{1,0:T(8,128)(2,1)} %param.16, f32[128,512]{1,0:T(8,128)} %fusion.55, bf16[128,512]{1,0:T(8,128)(2,1)S(1)} %copy-done.19, f32[128,512]{1,0:T(8,128)S(1)} %fusion.19, f32[128]{0:T(128)} %get-tuple-element.13, ...), kind=kOutput, calls=%fused_computation.79 | convolution fusion | flops 271515648 | bytes 4066304 | tf_op jit(solution)/shard_map/transpose(jvp())/dot_general | solution.py:13
  33.8 2.1 convolution_add_fusion.4
  36.0 3.2 %fusion.52 = f32[128,512]{1,0:T(8,128)} fusion(bf16[512,1024]{1,0:T(8,128)(2,1)S(1)} %copy-done, f32[128,1024]{1,0:T(8,128)} %copy-done.15, bf16[1024,512]{1,0:T(8,128)(2,1)} %param.16, f32[128,512]{1,0:T(8,128)} %copy-done.41, f32[128,512]{1,0:T(8,128)} %convolution_add_fusion.4, f32[128]{0:T(128)} %copy-done.25, f32[128]{0:T(128)} %copy-done.30, ...), kind=kOutput, calls=%fused_computation.76 | convolution fusion | flops 270729216 | bytes 3540992 | tf_op jit(solution)/shard_map/transpose(jvp())/dot_general | solution.py:13
  39.2 2.6 %fusion.4 = bf16[128,1024]{1,0:T(8,128)(2,1)} fusion(bf16[1024,512]{1,0:T(8,128)(2,1)} %param.14, f32[128,1024]{1,0:T(8,128)S(1)} %copy-done.7, f32[128,512]{1,0:T(8,128)} %convolution_add_fusion.4, f32[128]{0:T(128)} %copy-done.25, f32[128]{0:T(128)} %copy-done.27), kind=kOutput, calls=%fused_computation.12 | convolution fusion | flops 135593984 | bytes 2098176 | tf_op jit(solution)/shard_map/dot_general | solution.py:51
  41.8 1.9 fusion.276
  43.8 1.9 fusion.83
  45.6 2.8 %fusion.51 = f32[128,512]{1,0:T(8,128)S(1)} fusion(bf16[512,1024]{1,0:T(8,128)(2,1)S(1)} %copy-done, f32[128,1024]{1,0:T(8,128)} %copy-done.14, bf16[1024,512]{1,0:T(8,128)(2,1)} %param.16, f32[128,512]{1,0:T(8,128)} %copy-done.18, f32[128,512]{1,0:T(8,128)} %fusion.52, f32[128,512]{1,0:T(8,128)} %convolution_add_fusion.4, f32[128]{0:T(128)} %copy-done.32, ...), kind=kOutput, calls=%fused_computation.74 | convolution fusion | flops 271384576 | bytes 4328448 | tf_op jit(solution)/shard_map/transpose(jvp())/dot_general | solution.py:13
  48.9 4.0 %add_add_fusion = f32[512,1024]{1,0:T(8,128)} fusion(f32[512,1024]{1,0:T(8,128)} %fusion.83, f32[512,1024]{1,0:T(8,128)} %fusion.276, bf16[128,512]{1,0:T(8,128)(2,1)S(1)} %fusion.49, f32[128,1024]{1,0:T(8,128)S(1)} %convolution_add_fusion.2), kind=kOutput, calls=%fused_computation.1 | convolution fusion | flops 135921664 | bytes 6946816 | tf_op jit(solution)/shard_map/dot_general | solution.py:47
  53.1 1.4 fusion.242
  54.5 2.9 %fusion.237 = f32[512,1024]{1,0:T(8,128)} fusion(bf16[128,1024]{1,0:T(8,128)(2,1)} %copy-done.9, f32[128,512]{1,0:T(8,128)} %copy-done.3), kind=kOutput, calls=%fused_computation.250 | convolution fusion | flops 134283264 | bytes 2621440 | tf_op jit(solution)/shard_map/dot_general | solution.py:55
  57.3 4.3 %bitcast_add_fusion = f32[512,1024]{1,0:T(8,128)} fusion(f32[512,1024]{1,0:T(8,128)} %fusion.237, f32[512,1024]{1,0:T(8,128)S(1)} %fusion.242, bf16[128,512]{1,0:T(8,128)(2,1)} %param.11, bf16[128,512]{1,0:T(8,128)(2,1)S(1)} %fusion.49, bf16[1024,512]{1,0:T(8,128)(2,1)} %param.14, f32[128,1024]{1,0:T(8,128)} %copy-done.2), kind=kOutput, calls=%fused_computation | convolution fusion | flops 270663680 | bytes 8126464 | tf_op jit(solution)/shard_map/dot_general | solution.py:55
  61.7 55.7 %reduce-scatter.5.cloned.1.call-done = f32[32,1024]{1,0:T(8,128)} async-done(((f32[512,1024]{1,0:T(8,128)}), f32[32,1024]{1,0:T(8,128)}) %reduce-scatter.5.cloned.1.call-update) | async-done | bytes 131088 | tf_op jit(solution)/shard_map/reduce_scatter | solution.py:111
  117.4 64.9 %reduce-scatter.3.cloned.1.call-done = f32[32,1024]{1,0:T(8,128)} async-done(((f32[512,1024]{1,0:T(8,128)}), f32[32,1024]{1,0:T(8,128)}) %reduce-scatter.3.cloned.1.call-update) | async-done | bytes 131088 | tf_op jit(solution)/shard_map/reduce_scatter | solution.py:110
  182.3 2.0 pad_maximum_fusion
  184.2 40.0 %psum.21 = f32[3]{0:T(128)S(1)} all-reduce(f32[3]{0:T(128)S(1)} %pad_maximum_fusion), channel_id=1, replica_groups=mesh['grp'=2,'dp'=16] {'grp','dp'}, use_global_device_ids=true, to_apply=%region_3.4 | all-reduce | flops 3 | bytes 24 | tf_op jit(solution)/shard_map/psum | solution.py:100
  224.7 1.6 copy.18
  226.3 1.6 copy.19
  (109 shorter events, 10.4 us)
Async XLA Ops:
  7.2 5.4 %copy-start = (bf16[512,1024]{1,0:T(8,128)(2,1)S(1)}, bf16[512,1024]{1,0:T(8,128)(2,1)}, u32[]{:S(2)}) copy-start(bf16[512,1024]{1,0:T(8,128)(2,1)} %param.15) | copy-start | bytes 3145732
  7.2 110.2 %reduce-scatter.5.cloned.1.call-start = ((), (), s32[]{:S(2)}) async-start(), calls=%async_computation.3 | async-start | bytes 2228224 | tf_op jit(solution)/shard_map/reduce_scatter | solution.py:111
  8.0 13.7 %copy-start.25 = (f32[128]{0:T(128)}, f32[128]{0:T(128)S(1)}, u32[]{:S(2)}) copy-start(f32[128]{0:T(128)S(1)} %get-tuple-element.18) | copy-start | bytes 1540
  9.3 12.4 %copy-start.32 = (f32[128]{0:T(128)}, f32[128]{0:T(128)S(1)}, u32[]{:S(2)}) copy-start(f32[128]{0:T(128)S(1)} %get-tuple-element.14) | copy-start | bytes 1540
  10.1 11.6 %copy-start.27 = (f32[128]{0:T(128)}, f32[128]{0:T(128)S(1)}, u32[]{:S(2)}) copy-start(f32[128]{0:T(128)S(1)} %get-tuple-element.21) | copy-start | bytes 1540
  10.9 9.6 %copy-start.23 = (f32[128]{0:T(128)}, f32[128]{0:T(128)S(1)}, u32[]{:S(2)}) copy-start(f32[128]{0:T(128)S(1)} %get-tuple-element.8) | copy-start | bytes 1540
  11.0 10.8 %copy-start.21 = (f32[128]{0:T(128)}, f32[128]{0:T(128)S(1)}, u32[]{:S(2)}) copy-start(f32[128]{0:T(128)S(1)} %get-tuple-element.23) | copy-start | bytes 1540
  11.0 10.8 %copy-start.30 = (f32[128]{0:T(128)}, f32[128]{0:T(128)S(1)}, u32[]{:S(2)}) copy-start(f32[128]{0:T(128)S(1)} %get-tuple-element.22) | copy-start | bytes 1540
  12.5 36.4 %copy-start.2 = (f32[128,1024]{1,0:T(8,128)}, f32[128,1024]{1,0:T(8,128)S(1)}, u32[]{:S(2)}) copy-start(f32[128,1024]{1,0:T(8,128)S(1)} %convolution_add_fusion.2) | copy-start | bytes 1572868
  18.8 2.9 %copy-start.6 = (f32[128,1024]{1,0:T(8,128)}, f32[128,1024]{1,0:T(8,128)S(1)}, u32[]{:S(2)}) copy-start(f32[128,1024]{1,0:T(8,128)S(1)} %convolution_add_fusion.1) | copy-start | bytes 1572868
  20.5 4.1 %copy-start.18 = (f32[128,512]{1,0:T(8,128)}, f32[128,512]{1,0:T(8,128)S(1)}, u32[]{:S(2)}) copy-start(f32[128,512]{1,0:T(8,128)S(1)} %fusion.32) | copy-start | bytes 786436
  20.6 4.1 %copy-start.33 = (f32[128]{0:T(128)}, f32[128]{0:T(128)S(1)}, u32[]{:S(2)}) copy-start(f32[128]{0:T(128)S(1)} %get-tuple-element.29) | copy-start | bytes 1540
  21.7 3.0 %copy-start.41 = (f32[128,512]{1,0:T(8,128)}, f32[128,512]{1,0:T(8,128)S(1)}, u32[]{:S(2)}) copy-start(f32[128,512]{1,0:T(8,128)S(1)} %fusion.28) | copy-start | bytes 786436
  23.2 3.7 %copy-start.4 = (f32[128,1024]{1,0:T(8,128)}, f32[128,1024]{1,0:T(8,128)S(1)}, u32[]{:S(2)}) copy-start(f32[128,1024]{1,0:T(8,128)S(1)} %convolution_add_fusion) | copy-start | bytes 1572868
  24.7 2.2 copy-start.17
  27.4 6.4 %copy-start.9 = (bf16[128,1024]{1,0:T(8,128)(2,1)}, bf16[128,1024]{1,0:T(8,128)(2,1)S(1)}, u32[]{:S(2)}) copy-start(bf16[128,1024]{1,0:T(8,128)(2,1)S(1)} %fusion.5) | copy-start | bytes 786436
  35.9 3.2 %copy-start.7 = (f32[128,1024]{1,0:T(8,128)S(1)}, f32[128,1024]{1,0:T(8,128)}, u32[]{:S(2)}) copy-start(f32[128,1024]{1,0:T(8,128)} %copy-done.6) | copy-start | bytes 1572868
  39.2 2.6 %copy-start.8 = (f32[128,1024]{1,0:T(8,128)S(1)}, f32[128,1024]{1,0:T(8,128)}, u32[]{:S(2)}) copy-start(f32[128,1024]{1,0:T(8,128)} %copy-done.6) | copy-start | bytes 1572868
  39.2 2.6 %copy-start.11 = (f32[128,512]{1,0:T(8,128)S(1)}, f32[128,512]{1,0:T(8,128)}, u32[]{:S(2)}) copy-start(f32[128,512]{1,0:T(8,128)} %convolution_add_fusion.4) | copy-start | bytes 786436
  39.2 2.6 %copy-start.26 = (f32[128]{0:T(128)S(1)}, f32[128]{0:T(128)}, u32[]{:S(2)}) copy-start(f32[128]{0:T(128)} %copy-done.25) | copy-start | bytes 1540
  39.2 2.6 %copy-start.29 = (f32[128]{0:T(128)S(1)}, f32[128]{0:T(128)}, u32[]{:S(2)}) copy-start(f32[128]{0:T(128)} %copy-done.27) | copy-start | bytes 1540
  45.6 2.8 %copy-start.10 = (bf16[128,1024]{1,0:T(8,128)(2,1)S(1)}, bf16[128,1024]{1,0:T(8,128)(2,1)}, u32[]{:S(2)}) copy-start(bf16[128,1024]{1,0:T(8,128)(2,1)} %fusion.4) | copy-start | bytes 786436
  53.0 129.2 %reduce-scatter.3.cloned.1.call-start = ((), (), s32[]{:S(2)}) async-start(), calls=%async_computation.2 | async-start | bytes 2228224 | tf_op jit(solution)/shard_map/reduce_scatter | solution.py:110
  61.6 163.1 %all-reduce.3.cloned.1.call-start = ((), (), s32[]{:S(2)}) async-start(), calls=%async_computation.4 | async-start | bytes 524288 | tf_op jit(solution)/shard_map/psum | solution.py:113
  (21 other events, 29.7 us)
Sparse Core Ops, SparseCore 0:
  53.1 64.2 reduce-scatter.4
  121.6 60.6 reduce-scatter.2
  184.6 22.4 all-reduce.2
where the time goes:
time: 235 us; the launch traced here: 234 us
  waiting for transfers between devices  121 us (51%)
  matrix products  47.2 us (20%)
  blocking collectives  40 us (17%)
  between operations  14.3 us (6%)
  other arithmetic  6.19 us (3%)
  local copies, waits for them, and re-layouts  6.02 us (3%)
    reduce_scatter x1, waiting for transfers between devices, per_device(): lax.psum_scatter(grad_up, 'dp', scatter_dimension=0, tiled=True)  64.9 us
    reduce_scatter x1, waiting for transfers between devices, per_device(): lax.psum_scatter(grad_down, 'dp', scatter_dimension=0, tiled=True)  55.7 us
    psum x1, blocking collectives, per_device(): totals = lax.psum(jnp.stack(err_sums), ('grp', 'dp'))  40 us
    dot_general x8, matrix products, diffuse(): jnp.dot(current.astype(jnp.bfloat16), w_first, preferred_element_type=jnp...  13.7 us
    dot_general x3, matrix products, backward_step(): lax.dot_general(low_state, cot_pre, (((0,), (0,)), ((), ())), preferred_e...  8.52 us
    dot_general x3, matrix products, backward_step(): lax.dot_general(cot_drift, hidden, (((0,), (0,)), ((), ())), preferred_el...  7.85 us
    dot_general x6, matrix products, diffuse(): jnp.dot(inner.astype(jnp.bfloat16), w_second, preferred_element_type=jnp....  7.02 us
    unnamed x86, local copies, waits for them, and re-layouts  6.02 us
  transfers between devices with their start and end apart: 3, of which 2 were waited for; matrix products, arithmetic and copies ran while one was open for 5% of the time, Pallas kernels for 0%

commit v1 on v0

v1 whole, which is shorter than its diff:
```python
import functools

import jax
import jax.numpy as jnp
from jax import lax
from jax.experimental import pallas as pl
from jax.experimental.pallas import tpu as pltpu
from jax.sharding import PartitionSpec as P

base_step = 0.05
abs_tol = 0.01
rel_tol = 0.01
cores = 2
inner = 2
MESH = pl.DeviceIdType.MESH
f32 = jnp.float32
bf16 = jnp.bfloat16


def sigmoid(x):
    return 0.5 * jnp.tanh(0.5 * x) + 0.5


def dot(a, b):
    return jnp.dot(a, b, preferred_element_type=f32)


def dot_t(a, b):
    return lax.dot_general(a, b, (((1,), (1,)), ((), ())), preferred_element_type=f32)


def blocks(extent, width=256):
    width = min(width, extent)
    return [slice(at, at + width) for at in range(0, extent, width)]


def silu_pair(x):
    s = sigmoid(x)
    y = x * s
    return y.astype(bf16), s + y * (1.0 - s)


def prepare(ins, work):
    steps, rows = ins["mults"].shape
    table = work["table"]
    table[...] = jnp.zeros_like(table)
    table[0:steps, :] = ins["mults"][...].astype(f32) * base_step
    table[steps : 2 * steps, :] = ins["flags"][...].astype(f32)
    turned = table[...].T
    lanes = table.shape[0]
    for n in range(steps):
        h = jnp.broadcast_to(turned[:, n : n + 1], (rows, lanes))
        work["h"][n] = h
        work["r"][n] = jnp.sqrt(h)
        work["keep"][n] = jnp.broadcast_to(turned[:, steps + n : steps + n + 1], (rows, lanes))
    work["cur"][...] = ins["start"][...].astype(f32)
    work["cot"][...] = ins["cot"][...].astype(f32)
    work["err"][...] = jnp.zeros_like(work["err"])


def forward(n, ins, work):
    rows, latent = work["cur"].shape
    hidden = ins["w_up"].shape[1]
    at = pl.ds(pl.multiple_of(n * rows, rows), rows)
    h = work["h"][n][:, 0:1]
    r = work["r"][n][:, 0:1]
    keep = work["keep"][n][:, 0:1]
    cur = work["cur"][...]
    low = cur.astype(bf16)
    work["low_t"][:, at] = cur.T.astype(bf16)
    for j in blocks(hidden):
        work["in1"][:, j], work["d_in1"][n, :, j] = silu_pair(dot(low, ins["w_spread"][:, j]))
    for j in blocks(hidden):
        x = dot(low, ins["w_up"][:, j]) + ins["b_up"][:, j]
        work["hid"][at, j], work["d_hid"][n, :, j] = silu_pair(x)
    for j in blocks(latent):
        s = sigmoid(dot(work["in1"][...], ins["w_scale"][:, j]) + ins["b_scale"][:, j])
        g = 0.6 * s
        work["g"][:, j] = g
        work["d_g1"][n, :, j] = g * (1.0 - s)
        work["low2"][:, j] = (work["cur"][:, j] + g * r).astype(bf16)
    for j in blocks(hidden):
        work["in2"][:, j], work["d_in2"][n, :, j] = silu_pair(
            dot(work["low2"][...], ins["w_spread"][:, j])
        )
    total = jnp.zeros((1, 128), f32)
    for j in blocks(latent):
        s = sigmoid(dot(work["in2"][...], ins["w_scale"][:, j]) + ins["b_scale"][:, j])
        gbar = 0.6 * s
        work["d_g2"][n, :, j] = gbar * (1.0 - s)
        drift = dot(work["hid"][at, :], ins["w_down"][:, j])
        noise = ins["noise"][n, :, j].astype(f32)
        g = work["g"][:, j]
        c = work["cur"][:, j]
        milstein = (gbar - g) * (0.5 * r * (noise * noise - 1.0))
        scaled = milstein / (abs_tol + rel_tol * jnp.abs(c))
        part = jnp.sum(scaled * scaled, axis=0, keepdims=True)
        for i in blocks(part.shape[1], 128):
            total = total + part[:, i]
        proposal = c + drift * h + g * (r * noise) + milstein
        work["cur"][:, j] = jnp.where(keep > 0.5, proposal, c)
    work["err"][pl.ds(n, 1), :] = total


def back_drift(n, ins, work):
    rows, latent = work["cur"].shape
    at = pl.ds(pl.multiple_of(n * rows, rows), rows)
    cd = work["cot"][...] * (work["keep"][n][:, 0:1] * work["h"][n][:, 0:1])
    work["cd"][...] = cd.astype(bf16)
    work["cd_t"][:, at] = cd.T.astype(bf16)


def back_pre(n, ins, work):
    rows, latent = work["cur"].shape
    hidden = ins["w_up"].shape[1]
    at = pl.ds(pl.multiple_of(n * rows, rows), rows)
    for j in blocks(hidden):
        back = dot_t(work["cd"][...], ins["w_down"][j, :])
        work["cpre"][at, j] = (back * work["d_hid"][n, :, j]).astype(bf16)


def back_state(n, ins, work):
    rows, latent = work["cur"].shape
    hidden = ins["w_up"].shape[1]
    at = pl.ds(pl.multiple_of(n * rows, rows), rows)
    r = work["r"][n][:, 0:1]
    keep = work["keep"][n][:, 0:1]
    for j in blocks(latent):
        noise = ins["noise"][n, :, j].astype(f32)
        ck = keep * work["cot"][:, j]
        to_bar = ck * (0.5 * r * (noise * noise - 1.0))
        work["to_g"][:, j] = ck * (r * noise) - to_bar
        work["d_out"][:, j] = (to_bar * work["d_g2"][n, :, j]).astype(bf16)
    for j in blocks(hidden):
        back = dot_t(work["d_out"][...], ins["w_scale"][j, :]).astype(bf16).astype(f32)
        work["in2"][:, j] = (back * work["d_in2"][n, :, j]).astype(bf16)
    for j in blocks(latent):
        back = dot_t(work["in2"][...], ins["w_spread"][j, :]).astype(bf16).astype(f32)
        work["g"][:, j] = back
        work["d_out"][:, j] = (
            (work["to_g"][:, j] + back * r) * work["d_g1"][n, :, j]
        ).astype(bf16)
    for j in blocks(hidden):
        back = dot_t(work["d_out"][...], ins["w_scale"][j, :]).astype(bf16).astype(f32)
        work["in1"][:, j] = (back * work["d_in1"][n, :, j]).astype(bf16)
    for j in blocks(latent):
        back = dot_t(work["in1"][...], ins["w_spread"][j, :]).astype(bf16).astype(f32)
        through = dot_t(work["cpre"][at, :], ins["w_up"][j, :])
        work["cot"][:, j] = work["cot"][:, j] + work["g"][:, j] + back + through


names = (
    "start", "w_up", "b_up", "w_down", "w_spread", "w_scale", "b_scale", "noise", "mults",
    "flags", "cot",
)


def work_shapes(steps, rows, latent, hidden):
    vm = pltpu.VMEM
    return dict(
        table=vm((128, rows), f32),
        h=vm((steps, rows, 128), f32),
        r=vm((steps, rows, 128), f32),
        keep=vm((steps, rows, 128), f32),
        cur=vm((rows, latent), f32),
        cot=vm((rows, latent), f32),
        err=vm((8, 128), f32),
        low_t=vm((latent, steps * rows), bf16),
        cd_t=vm((latent, steps * rows), bf16),
        hid=vm((steps * rows, hidden), bf16),
        cpre=vm((steps * rows, hidden), bf16),
        d_hid=vm((steps, rows, hidden), f32),
        in1=vm((rows, hidden), bf16),
        d_in1=vm((steps, rows, hidden), f32),
        in2=vm((rows, hidden), bf16),
        d_in2=vm((steps, rows, hidden), f32),
        g=vm((rows, latent), f32),
        d_g1=vm((steps, rows, latent), f32),
        d_g2=vm((steps, rows, latent), f32),
        low2=vm((rows, latent), bf16),
        cd=vm((rows, latent), bf16),
        to_g=vm((rows, latent), f32),
        d_out=vm((rows, latent), bf16),
    )


def local_kernel(work_names, *refs):
    ins = dict(zip(names, refs))
    err_ref, up_ref, down_ref = refs[len(names) : len(names) + 3]
    work = dict(zip(work_names, refs[len(names) + 3 :]))
    steps = ins["mults"].shape[0]
    prepare(ins, work)

    @pl.loop(0, steps)
    def _(n):
        forward(n, ins, work)

    err_ref[...] = work["err"][...]

    @pl.loop(0, steps - 1)
    def _(i):
        n = steps - 1 - i
        back_drift(n, ins, work)
        back_pre(n, ins, work)
        back_state(n, ins, work)

    back_drift(0, ins, work)
    back_pre(0, ins, work)
    for j in blocks(down_ref.shape[1]):
        down_ref[:, j] = dot(work["cd_t"][...], work["hid"][:, j])
        up_ref[:, j] = dot(work["low_t"][...], work["cpre"][:, j])


def whole_kernel(work_names, groups, members, total_count, *refs):
    ins = dict(zip(names, refs))
    err_ref, up_ref, down_ref = refs[len(names) : len(names) + 3]
    work = dict(zip(work_names, refs[len(names) + 3 :]))
    steps = ins["mults"].shape[0]
    latent, hidden = ins["w_up"].shape
    outer = members // (inner * cores)
    chunk = latent // members
    half = chunk // groups
    x = lax.axis_index("grp")
    place = lax.axis_index("dp")
    core = lax.rem(place, cores)
    y = lax.rem(place // cores, inner)
    z = place // (cores * inner)

    def at(g, o, i, c):
        return (g, (o * inner + i) * cores + c)

    mate = at(x, z, y, 1 - core)
    beside = at(x, z, 1 - y, core)
    across = at(1 - x, z, y, core)
    along = [at(x, lax.rem(z + 1 + k, outer), y, core) for k in range(outer - 1)]
    partners = [mate, beside, across] + along

    barrier = pltpu.get_barrier_semaphore()
    for partner in partners:
        pl.semaphore_signal(barrier, inc=1, device_id=partner, device_id_type=MESH)

    pending = {}

    def send(key, source, target, device):
        number = len(pending)
        pending[key] = pltpu.make_async_remote_copy(
            src_ref=source,
            dst_ref=target,
            send_sem=work["sent"].at[number],
            recv_sem=work["got"].at[number],
            device_id=device,
            device_id_type=MESH,
        )
        pending[key].start()

    prepare(ins, work)

    @pl.loop(0, steps)
    def _(n):
        forward(n, ins, work)

    pl.semaphore_wait(barrier, len(partners))
    err_in = work["err_in"]
    err_sum = work["err_sum"]
    send("e0", work["err"], err_in.at[0], mate)

    @pl.loop(0, steps - 1)
    def _(i):
        n = steps - 1 - i
        back_drift(n, ins, work)
        back_pre(n, ins, work)
        back_state(n, ins, work)

    pending["e0"].wait_recv()
    err_sum[0] = work["err"][...] + err_in[0]
    send("e1", err_sum.at[0], err_in.at[1], beside)
    back_drift(0, ins, work)

    grads = work["grads"]
    in0, in1, in2, in3, in4 = (work[f"arrive{i}"] for i in range(5))
    mine = pl.ds(pl.multiple_of(x * half, half), half)
    other = pl.ds(pl.multiple_of((1 - x) * half, half), half)
    span = latent // outer

    def product(a, k):
        left, right = (("cd_t", "hid"), ("low_t", "cpre"))[a]
        piece = lax.rem(z + 1 + k, outer)
        rows = pl.ds(pl.multiple_of(piece * span, span), span)
        for j in blocks(hidden):
            value = dot(work[left][rows, :], work[right][:, j])
            grads[a, k, :, :, :, j] = value.reshape(inner, cores, chunk, value.shape[1])
        send((0, a, k), grads.at[a, k, :, 1 - core], in0.at[a, k], mate)

    def first(a, k):
        pending[0, a, k].wait_recv()
        grads[a, k, :, core] = grads[a, k, :, core] + in0[a, k]
        if a == 0:
            send((1, a, k), grads.at[a, k, 1 - y, core], in1.at[k], beside)
        else:
            send((1, a, k), grads.at[a, k, :, core, other], work["arrive1b"].at[k], across)

    def second(a, k):
        pending[1, a, k].wait_recv()
        if a == 0:
            grads[a, k, y, core] = grads[a, k, y, core] + in1[k]
            send((2, a, k), grads.at[a, k, y, core, other], in2.at[a, k], across)
        else:
            grads[a, k, :, core, mine] = grads[a, k, :, core, mine] + work["arrive1b"][k]
            send((2, a, k), grads.at[a, k, 1 - y, core, mine], in2.at[a, k], beside)

    def third(a, k):
        pending[2, a, k].wait_recv()
        grads[a, k, y, core, mine] = grads[a, k, y, core, mine] + in2[a, k]
        if k < outer - 1:
            send((3, a, k), grads.at[a, k, y, core, mine], in3.at[a, k], along[k])

    def fourth(a):
        value = grads[a, outer - 1, y, core, mine]
        for k in range(outer - 1):
            pending[3, a, k].wait_recv()
            value = value + in3[a, k]
        work["done"][a] = value
        send((4, a), work["done"].at[a], in4.at[a], across)
        (down_ref, up_ref)[a][mine, :] = value

    def fifth(a):
        pending[4, a].wait_recv()
        (down_ref, up_ref)[a][other, :] = in4[a]

    for k in range(outer):
        product(0, k)
    first(0, 0)
    back_pre(0, ins, work)
    for k in range(1, outer):
        first(0, k)
    for k in range(outer):
        product(1, k)
        if k > 0:
            first(1, k - 1)
    first(1, outer - 1)
    pending["e1"].wait_recv()
    err_sum[1] = err_sum[0] + err_in[1]
    send("e2", err_sum.at[1], err_in.at[2], across)
    for k in range(outer):
        second(0, k)
        second(1, k)
        if k == 1:
            pending["e2"].wait_recv()
            err_sum[2] = err_sum[1] + err_in[2]
            for i in range(outer - 1):
                send(("e3", i), err_sum.at[2], err_in.at[3 + i], along[i])
        if k > 0:
            third(0, k - 1)
            third(1, k - 1)
    third(0, outer - 1)
    third(1, outer - 1)
    fourth(0)
    fourth(1)
    total = err_sum[2]
    for i in range(outer - 1):
        pending["e3", i].wait_recv()
        total = total + err_in[3 + i]
    norms = jnp.sqrt(jnp.sum(total, axis=1, keepdims=True) * (1.0 / total_count))
    for n in range(steps):
        err_ref[n] = jnp.sum(norms[n : n + 1, 0:1])
    fifth(0)
    fifth(1)
    for copy in pending.values():
        copy.wait_send()


def per_device(
    start_state, w_up, b_up, w_down, w_spread, w_scale, b_scale, brownian_noise, step_mults,
    accept_flags, cotangent,
):
    groups = lax.axis_size("grp")
    members = lax.axis_size("dp")
    rows, latent = start_state.shape
    hidden = w_up.shape[1]
    steps = brownian_noise.shape[0]
    total_count = rows * latent * groups * members
    args = (
        start_state, w_up, b_up[None, :], w_down, w_spread, w_scale, b_scale[None, :],
        brownian_noise, step_mults, accept_flags, cotangent,
    )
    work = work_shapes(steps, rows, latent, hidden)
    vmem = pl.BlockSpec(memory_space=pltpu.VMEM)
    chunk = latent // members
    paired = groups == 2 and members % (inner * cores) == 0 and members > inner * cores
    if not paired or chunk % (8 * groups) != 0:
        err, up, down = pl.pallas_call(
            functools.partial(local_kernel, tuple(work)),
            out_shape=(
                jax.ShapeDtypeStruct((8, 128), f32),
                jax.ShapeDtypeStruct((latent, hidden), f32),
                jax.ShapeDtypeStruct((latent, hidden), f32),
            ),
            in_specs=[vmem] * len(args),
            out_specs=(vmem,) * 3,
            scratch_shapes=list(work.values()),
            compiler_params=pltpu.CompilerParams(vmem_limit_bytes=56 * 2**20),
        )(*args)
        totals = lax.psum(jnp.sum(err[:steps], axis=1), ("grp", "dp"))
        up, down = (
            lax.psum_scatter(g, "dp", scatter_dimension=0, tiled=True) for g in (up, down)
        )
        up, down = lax.psum((up, down), "grp")
        return (jnp.sqrt(totals / total_count), up, down)
    outer = members // (inner * cores)
    half = chunk // groups
    vm = pltpu.VMEM
    copies = 6 * outer + 2 * (outer - 1) + 2 + 3 + outer - 1
    work.update(
        grads=vm((2, outer, inner, cores, chunk, hidden), f32),
        arrive0=vm((2, outer, inner, chunk, hidden), f32),
        arrive1=vm((outer, chunk, hidden), f32),
        arrive1b=vm((outer, inner, half, hidden), f32),
        arrive2=vm((2, outer, half, hidden), f32),
        arrive3=vm((2, outer - 1, half, hidden), f32),
        arrive4=vm((2, half, hidden), f32),
        done=vm((2, half, hidden), f32),
        err_in=vm((2 + outer, 8, 128), f32),
        err_sum=vm((3, 8, 128), f32),
        sent=pltpu.SemaphoreType.DMA((copies,)),
        got=pltpu.SemaphoreType.DMA((copies,)),
    )
    return pl.pallas_call(
        functools.partial(whole_kernel, tuple(work), groups, members, total_count),
        out_shape=(
            jax.ShapeDtypeStruct((steps,), f32),
            jax.ShapeDtypeStruct((chunk, hidden), f32),
            jax.ShapeDtypeStruct((chunk, hidden), f32),
        ),
        in_specs=[vmem] * len(args),
        out_specs=(pl.BlockSpec(memory_space=pltpu.SMEM), vmem, vmem),
        scratch_shapes=list(work.values()),
        compiler_params=pltpu.CompilerParams(
            vmem_limit_bytes=56 * 2**20, collective_id=0, has_side_effects=True
        ),
    )(*args)


def solution(mesh):
    in_specs = (
        P(("grp", "dp"), None),
        P(),
        P(),
        P(),
        P(),
        P(),
        P(),
        P(None, ("grp", "dp"), None),
        P(None, ("grp", "dp")),
        P(None, ("grp", "dp")),
        P(("grp", "dp"), None),
    )
    out_specs = (P(), P("dp", None), P("dp", None))
    return jax.shard_map(
        per_device, mesh=mesh, in_specs=in_specs, out_specs=out_specs, check_vma=False
    )
```

time: 235 us -> 54 us (0.23)
  waiting for transfers between devices: 121 us -> 0 us
  Pallas kernels: 0 us -> 49.4 us
  matrix products: 47.2 us -> 0 us
  blocking collectives: 40 us -> 0 us
  between operations: 14.3 us -> 0.65 us
  other arithmetic: 6.19 us -> 0 us
  local copies, waits for them, and re-layouts: 6.02 us -> 3.44 us
    reduce_scatter x2 -> x0, waiting for transfers between devices: 121 us -> none  [the longest x1 64.9 us: per_device(): lax.psum_scatter(grad_up, 'dp', scatter_dimension=0, tiled=True)]
    pallas_call x0 -> x1, Pallas kernels: none -> 49.4 us  [per_device(): pl.pallas_call(functools.partial(whole_kernel, tuple(work), groups, membe...]
    dot_general x29 -> x0, matrix products: 47.2 us -> none  [the longest x8 13.7 us: diffuse(): jnp.dot(current.astype(jnp.bfloat16), w_first, preferred_element_type=jnp...]
    psum x1 -> x0, blocking collectives: 40 us -> none  [per_device(): totals = lax.psum(jnp.stack(err_sums), ('grp', 'dp'))]
    unnamed x86 -> x7, local copies, waits for them, and re-layouts: 6.02 us -> 3.44 us
  transfers between devices with their start and end apart: 3 -> 0, of which waited for: 2 -> 0; matrix products, arithmetic and copies ran while one was open for 5% -> 0% of each run, Pallas kernels for 0% -> 0%
where the time goes in v1:
time: 54 us; the launch traced here: 53.4 us
  Pallas kernels  49.4 us (91%)
  local copies, waits for them, and re-layouts  3.44 us (6%)
  between operations  0.65 us (1%)
    pallas_call x1, Pallas kernels, per_device(): pl.pallas_call(functools.partial(whole_kernel, tuple(work), groups, membe...  49.4 us
    unnamed x7, local copies, waits for them, and re-layouts  3.44 us

profile of v1, /device:TPU:0, one launch (start us, length us, event | category | flops | bytes accessed | tf_op | source)
XLA Modules:
  0.0 53.4 jit_solution(17825410735143653064)
XLA Ops:
  0.6 49.4 %shard_map.130 = (f32[3]{0:T(128)}, f32[32,1024]{1,0:T(8,128)}, f32[32,1024]{1,0:T(8,128)}) custom-call(bf16[128,512]{1,0:T(8,128)(2,1)} %refs_0_.1, bf16[512,1024]{1,0:T(8,128)(2,1)} %refs_1_.1, f32[1,1024]{1,0:T(1,128)} %bitcast.2, bf16[1024,512]{1,0:T(8,128)(2,1)} %refs_3_.1, bf16[512,1024]{1,0:T(8,128)(2,1)} %refs_4_.1, bf16[1024,512]{1,0:T(8,128)(2,1)} %refs_5_.1, ...), custom_call_target="tpu_custom_call" | custom-call | tf_op jit(solution)/shard_map/pallas_call | solution.py:427
  50.0 0.0 copy-start.1
  50.0 0.7 %copy-done.1 = f32[3]{0:T(128)S(1)} copy-done((f32[3]{0:T(128)S(1)}, f32[3]{0:T(128)}, u32[]{:S(2)}) %copy-start.1) | copy-done | bytes 36
  50.7 0.5 copy.17
  51.2 0.0 copy-start
  51.2 1.6 %copy.18 = f32[32,1024]{1,0:T(8,128)} copy(f32[32,1024]{1,0:T(8,128)} %get-tuple-element.7) | data formatting | bytes 262144
  52.8 0.0 copy-done
  52.8 0.7 %copy.19 = f32[32,1024]{1,0:T(8,128)} copy(f32[32,1024]{1,0:T(8,128)S(1)} %copy-done) | data formatting | bytes 262144
Async XLA Ops:
  50.0 0.7 %copy-start.1 = (f32[3]{0:T(128)S(1)}, f32[3]{0:T(128)}, u32[]{:S(2)}) copy-start(f32[3]{0:T(128)} %get-tuple-element.6) | copy-start | bytes 40
  51.2 1.6 %copy-start = (f32[32,1024]{1,0:T(8,128)S(1)}, f32[32,1024]{1,0:T(8,128)}, u32[]{:S(2)}) copy-start(f32[32,1024]{1,0:T(8,128)} %get-tuple-element.8) | copy-start | bytes 393220

commit v2 on v1

--- a/solution.py
+++ b/solution.py
@@ -278,6 +278,7 @@
 
     grads = work["grads"]
     in0, in1, in2, in3, in4 = (work[f"arrive{i}"] for i in range(5))
+    in1b = work["arrive1b"]
     mine = pl.ds(pl.multiple_of(x * half, half), half)
     other = pl.ds(pl.multiple_of((1 - x) * half, half), half)
     span = latent // outer
@@ -291,21 +292,24 @@
             grads[a, k, :, :, :, j] = value.reshape(inner, cores, chunk, value.shape[1])
         send((0, a, k), grads.at[a, k, :, 1 - core], in0.at[a, k], mate)
 
+    def y_first(a, k):
+        return (a == 0) if k == outer - 1 else (a + k) % 2 == 0
+
     def first(a, k):
         pending[0, a, k].wait_recv()
         grads[a, k, :, core] = grads[a, k, :, core] + in0[a, k]
-        if a == 0:
-            send((1, a, k), grads.at[a, k, 1 - y, core], in1.at[k], beside)
+        if y_first(a, k):
+            send((1, a, k), grads.at[a, k, 1 - y, core], in1.at[a, k], beside)
         else:
-            send((1, a, k), grads.at[a, k, :, core, other], work["arrive1b"].at[k], across)
+            send((1, a, k), grads.at[a, k, :, core, other], in1b.at[a, k], across)
 
     def second(a, k):
         pending[1, a, k].wait_recv()
-        if a == 0:
-            grads[a, k, y, core] = grads[a, k, y, core] + in1[k]
+        if y_first(a, k):
+            grads[a, k, y, core] = grads[a, k, y, core] + in1[a, k]
             send((2, a, k), grads.at[a, k, y, core, other], in2.at[a, k], across)
         else:
-            grads[a, k, :, core, mine] = grads[a, k, :, core, mine] + work["arrive1b"][k]
+            grads[a, k, :, core, mine] = grads[a, k, :, core, mine] + in1b[a, k]
             send((2, a, k), grads.at[a, k, 1 - y, core, mine], in2.at[a, k], beside)
 
     def third(a, k):
@@ -327,33 +331,34 @@
         pending[4, a].wait_recv()
         (down_ref, up_ref)[a][other, :] = in4[a]
 
+    order = [(0, k) for k in range(outer - 1)] + [(1, k) for k in range(outer - 1)]
+    order += [(0, outer - 1), (1, outer - 1)]
     for k in range(outer):
         product(0, k)
-    first(0, 0)
+    first(*order[0])
+    first(*order[1])
     back_pre(0, ins, work)
-    for k in range(1, outer):
-        first(0, k)
     for k in range(outer):
         product(1, k)
-        if k > 0:
-            first(1, k - 1)
-    first(1, outer - 1)
     pending["e1"].wait_recv()
     err_sum[1] = err_sum[0] + err_in[1]
     send("e2", err_sum.at[1], err_in.at[2], across)
-    for k in range(outer):
-        second(0, k)
-        second(1, k)
-        if k == 1:
+    count = len(order)
+    for at_pair in range(2, count + 4, 2):
+        for i in (at_pair, at_pair + 1):
+            if i < count:
+                first(*order[i])
+        for i in (at_pair - 2, at_pair - 1):
+            if i < count:
+                second(*order[i])
+        for i in (at_pair - 4, at_pair - 3):
+            if 0 <= i < count:
+                third(*order[i])
+        if at_pair == 4:
             pending["e2"].wait_recv()
             err_sum[2] = err_sum[1] + err_in[2]
             for i in range(outer - 1):
                 send(("e3", i), err_sum.at[2], err_in.at[3 + i], along[i])
-        if k > 0:
-            third(0, k - 1)
-            third(1, k - 1)
-    third(0, outer - 1)
-    third(1, outer - 1)
     fourth(0)
     fourth(1)
     total = err_sum[2]
@@ -367,6 +372,19 @@
     fifth(1)
     for copy in pending.values():
         copy.wait_send()
+
+
+def hand_over(err_ref, up_ref, down_ref, err_out, up_out, down_out, sems):
+    copies = [
+        pltpu.make_async_copy(up_ref, up_out, sems.at[0]),
+        pltpu.make_async_copy(down_ref, down_out, sems.at[1]),
+    ]
+    for copy in copies:
+        copy.start()
+    for n in range(err_out.shape[0]):
+        err_out[n] = err_ref[n]
+    for copy in copies:
+        copy.wait()
 
 
 def per_device(
@@ -413,8 +431,8 @@
     work.update(
         grads=vm((2, outer, inner, cores, chunk, hidden), f32),
         arrive0=vm((2, outer, inner, chunk, hidden), f32),
-        arrive1=vm((outer, chunk, hidden), f32),
-        arrive1b=vm((outer, inner, half, hidden), f32),
+        arrive1=vm((2, outer, chunk, hidden), f32),
+        arrive1b=vm((2, outer, inner, half, hidden), f32),
         arrive2=vm((2, outer, half, hidden), f32),
         arrive3=vm((2, outer - 1, half, hidden), f32),
         arrive4=vm((2, half, hidden), f32),
@@ -424,13 +442,14 @@
         sent=pltpu.SemaphoreType.DMA((copies,)),
         got=pltpu.SemaphoreType.DMA((copies,)),
     )
-    return pl.pallas_call(
+    out_shape = (
+        jax.ShapeDtypeStruct((steps,), f32),
+        jax.ShapeDtypeStruct((chunk, hidden), f32),
+        jax.ShapeDtypeStruct((chunk, hidden), f32),
+    )
+    results = pl.pallas_call(
         functools.partial(whole_kernel, tuple(work), groups, members, total_count),
-        out_shape=(
-            jax.ShapeDtypeStruct((steps,), f32),
-            jax.ShapeDtypeStruct((chunk, hidden), f32),
-            jax.ShapeDtypeStruct((chunk, hidden), f32),
-        ),
+        out_shape=out_shape,
         in_specs=[vmem] * len(args),
         out_specs=(pl.BlockSpec(memory_space=pltpu.SMEM), vmem, vmem),
         scratch_shapes=list(work.values()),
@@ -438,6 +457,16 @@
             vmem_limit_bytes=56 * 2**20, collective_id=0, has_side_effects=True
         ),
     )(*args)
+    smem = pl.BlockSpec(memory_space=pltpu.SMEM)
+    anywhere = pl.BlockSpec(memory_space=pl.ANY)
+    return pl.pallas_call(
+        hand_over,
+        out_shape=out_shape,
+        in_specs=[smem, anywhere, anywhere],
+        out_specs=(smem, anywhere, anywhere),
+        scratch_shapes=[pltpu.SemaphoreType.DMA((2,))],
+        compiler_params=pltpu.CompilerParams(vmem_limit_bytes=60 * 2**20),
+    )(*results)
 
 
 def solution(mesh):

time: 54 us -> 55.8 us (1.033)
  Pallas kernels: 49.4 us -> 55 us
  local copies, waits for them, and re-layouts: 3.44 us -> 0 us
    pallas_call x0 -> x1, Pallas kernels: none -> 10.2 us  [per_device(): pl.pallas_call(hand_over, out_shape=out_shape, in_specs=[smem, anywhere,...]
    pallas_call x1, Pallas kernels: 49.4 us -> 44.8 us  [per_device(): pl.pallas_call(functools.partial(whole_kernel, tuple(work), groups, membe...]
    unnamed x7 -> x0, local copies, waits for them, and re-layouts: 3.44 us -> none
where the time goes in v2:
time: 55.8 us; the launch traced here: 55.6 us
  Pallas kernels  55 us (99%)
  between operations  0.64 us (1%)
    pallas_call x1, Pallas kernels, per_device(): pl.pallas_call(functools.partial(whole_kernel, tuple(work), groups, membe...  44.8 us
    pallas_call x1, Pallas kernels, per_device(): pl.pallas_call(hand_over, out_shape=out_shape, in_specs=[smem, anywhere,...  10.2 us

profile of v2, /device:TPU:0, one launch (start us, length us, event | category | flops | bytes accessed | tf_op | source)
XLA Modules:
  0.0 55.6 jit_solution(6764349841566295349)
XLA Ops:
  0.6 44.8 %shard_map.130 = (f32[3]{0:T(128)}, f32[32,1024]{1,0:T(8,128)}, f32[32,1024]{1,0:T(8,128)}) custom-call(bf16[128,512]{1,0:T(8,128)(2,1)} %refs_0_.1, bf16[512,1024]{1,0:T(8,128)(2,1)} %refs_1_.1, f32[1,1024]{1,0:T(1,128)} %bitcast.2, bf16[1024,512]{1,0:T(8,128)(2,1)} %refs_3_.1, bf16[512,1024]{1,0:T(8,128)(2,1)} %refs_4_.1, bf16[1024,512]{1,0:T(8,128)(2,1)} %refs_5_.1, ...), custom_call_target="tpu_custom_call" | custom-call | tf_op jit(solution)/shard_map/pallas_call | solution.py:450
  45.4 10.2 %shard_map.131 = (f32[3]{0:T(128)}, f32[32,1024]{1,0:T(8,128)}, f32[32,1024]{1,0:T(8,128)}) custom-call(f32[3]{0:T(128)} %get-tuple-element.6.err_ref, f32[32,1024]{1,0:T(8,128)} %get-tuple-element.7.up_ref, f32[32,1024]{1,0:T(8,128)} %get-tuple-element.8.down_ref), custom_call_target="tpu_custom_call" | custom-call | tf_op jit(solution)/shard_map/pallas_call | solution.py:462

commit v3 on v2

--- a/solution.py
+++ b/solution.py
@@ -374,17 +374,11 @@
         copy.wait_send()
 
 
-def hand_over(err_ref, up_ref, down_ref, err_out, up_out, down_out, sems):
-    copies = [
-        pltpu.make_async_copy(up_ref, up_out, sems.at[0]),
-        pltpu.make_async_copy(down_ref, down_out, sems.at[1]),
-    ]
-    for copy in copies:
-        copy.start()
+def hand_over(err_ref, up_ref, down_ref, err_out, up_out, down_out):
+    up_out[...] = up_ref[...]
+    down_out[...] = down_ref[...]
     for n in range(err_out.shape[0]):
         err_out[n] = err_ref[n]
-    for copy in copies:
-        copy.wait()
 
 
 def per_device(
@@ -458,13 +452,11 @@
         ),
     )(*args)
     smem = pl.BlockSpec(memory_space=pltpu.SMEM)
-    anywhere = pl.BlockSpec(memory_space=pl.ANY)
     return pl.pallas_call(
         hand_over,
         out_shape=out_shape,
-        in_specs=[smem, anywhere, anywhere],
-        out_specs=(smem, anywhere, anywhere),
-        scratch_shapes=[pltpu.SemaphoreType.DMA((2,))],
+        in_specs=[smem, vmem, vmem],
+        out_specs=(smem, vmem, vmem),
         compiler_params=pltpu.CompilerParams(vmem_limit_bytes=60 * 2**20),
     )(*results)
 

time: 55.8 us -> 47.3 us (0.85)
  Pallas kernels: 55 us -> 46.5 us
    pallas_call x1, Pallas kernels: 10.2 us -> 1.69 us  [per_device(): pl.pallas_call(hand_over, out_shape=out_shape, in_specs=[smem, vmem, vmem...]
where the time goes in v3:
time: 47.3 us; the launch traced here: 47.1 us
  Pallas kernels  46.5 us (98%)
  between operations  0.64 us (1%)
    pallas_call x1, Pallas kernels, per_device(): pl.pallas_call(functools.partial(whole_kernel, tuple(work), groups, membe...  44.8 us
    pallas_call x1, Pallas kernels, per_device(): pl.pallas_call(hand_over, out_shape=out_shape, in_specs=[smem, vmem, vmem...  1.69 us

profile of v3, /device:TPU:0, one launch (start us, length us, event | category | flops | bytes accessed | tf_op | source)
XLA Modules:
  0.0 47.1 jit_solution(14533818931490007486)
XLA Ops:
  0.6 44.8 %shard_map.130 = (f32[3]{0:T(128)}, f32[32,1024]{1,0:T(8,128)}, f32[32,1024]{1,0:T(8,128)}) custom-call(bf16[128,512]{1,0:T(8,128)(2,1)} %refs_0_.1, bf16[512,1024]{1,0:T(8,128)(2,1)} %refs_1_.1, f32[1,1024]{1,0:T(1,128)} %bitcast.2, bf16[1024,512]{1,0:T(8,128)(2,1)} %refs_3_.1, bf16[512,1024]{1,0:T(8,128)(2,1)} %refs_4_.1, bf16[1024,512]{1,0:T(8,128)(2,1)} %refs_5_.1, ...), custom_call_target="tpu_custom_call" | custom-call | tf_op jit(solution)/shard_map/pallas_call | solution.py:444
  45.4 1.7 %shard_map.131 = (f32[3]{0:T(128)}, f32[32,1024]{1,0:T(8,128)}, f32[32,1024]{1,0:T(8,128)}) custom-call(f32[3]{0:T(128)} %get-tuple-element.6.err_ref, f32[32,1024]{1,0:T(8,128)} %get-tuple-element.7.up_ref, f32[32,1024]{1,0:T(8,128)} %get-tuple-element.8.down_ref), custom_call_target="tpu_custom_call" | custom-call | tf_op jit(solution)/shard_map/pallas_call | solution.py:455

commit v4 on v3

--- a/solution.py
+++ b/solution.py
@@ -58,6 +58,17 @@
     work["err"][...] = jnp.zeros_like(work["err"])
 
 
+late = ("w_up", "w_scale", "w_down", "noise")
+
+
+def ready(n, ins, name):
+    if "loads" in ins:
+
+        @pl.when(n == 0)
+        def _():
+            ins["loads"][name].wait()
+
+
 def forward(n, ins, work):
     rows, latent = work["cur"].shape
     hidden = ins["w_up"].shape[1]
@@ -70,9 +81,11 @@
     work["low_t"][:, at] = cur.T.astype(bf16)
     for j in blocks(hidden):
         work["in1"][:, j], work["d_in1"][n, :, j] = silu_pair(dot(low, ins["w_spread"][:, j]))
+    ready(n, ins, "w_up")
     for j in blocks(hidden):
         x = dot(low, ins["w_up"][:, j]) + ins["b_up"][:, j]
         work["hid"][at, j], work["d_hid"][n, :, j] = silu_pair(x)
+    ready(n, ins, "w_scale")
     for j in blocks(latent):
         s = sigmoid(dot(work["in1"][...], ins["w_scale"][:, j]) + ins["b_scale"][:, j])
         g = 0.6 * s
@@ -83,6 +96,8 @@
         work["in2"][:, j], work["d_in2"][n, :, j] = silu_pair(
             dot(work["low2"][...], ins["w_spread"][:, j])
         )
+    ready(n, ins, "w_down")
+    ready(n, ins, "noise")
     total = jnp.zeros((1, 128), f32)
     for j in blocks(latent):
         s = sigmoid(dot(work["in2"][...], ins["w_scale"][:, j]) + ins["b_scale"][:, j])
@@ -253,6 +268,12 @@
         )
         pending[key].start()
 
+    loads = {}
+    for i, name in enumerate(late):
+        loads[name] = pltpu.make_async_copy(ins[name], work[name], work["loaded"].at[i])
+        loads[name].start()
+        ins[name] = work[name]
+    ins["loads"] = loads
     prepare(ins, work)
 
     @pl.loop(0, steps)
@@ -435,6 +456,11 @@
         err_sum=vm((3, 8, 128), f32),
         sent=pltpu.SemaphoreType.DMA((copies,)),
         got=pltpu.SemaphoreType.DMA((copies,)),
+        loaded=pltpu.SemaphoreType.DMA((len(late),)),
+        w_up=vm(w_up.shape, bf16),
+        w_scale=vm(w_scale.shape, bf16),
+        w_down=vm(w_down.shape, bf16),
+        noise=vm(brownian_noise.shape, bf16),
     )
     out_shape = (
         jax.ShapeDtypeStruct((steps,), f32),
@@ -444,7 +470,7 @@
     results = pl.pallas_call(
         functools.partial(whole_kernel, tuple(work), groups, members, total_count),
         out_shape=out_shape,
-        in_specs=[vmem] * len(args),
+        in_specs=[pl.BlockSpec(memory_space=pl.ANY) if name in late else vmem for name in names],
         out_specs=(pl.BlockSpec(memory_space=pltpu.SMEM), vmem, vmem),
         scratch_shapes=list(work.values()),
         compiler_params=pltpu.CompilerParams(

time: 47.3 us -> 48.5 us (1.025)
  Pallas kernels: 46.5 us -> 47.7 us
    pallas_call x1, Pallas kernels: 44.8 us -> 46 us  [per_device(): pl.pallas_call(functools.partial(whole_kernel, tuple(work), groups, membe...]
where the time goes in v4:
time: 48.5 us; the launch traced here: 48.4 us
  Pallas kernels  47.7 us (98%)
  between operations  0.64 us (1%)
    pallas_call x1, Pallas kernels, per_device(): pl.pallas_call(functools.partial(whole_kernel, tuple(work), groups, membe...  46 us
    pallas_call x1, Pallas kernels, per_device(): pl.pallas_call(hand_over, out_shape=out_shape, in_specs=[smem, vmem, vmem...  1.69 us

profile of v4, /device:TPU:0, one launch (start us, length us, event | category | flops | bytes accessed | tf_op | source)
XLA Modules:
  0.0 48.4 jit_solution(10088669100703250029)
XLA Ops:
  0.6 46.0 %shard_map.130 = (f32[3]{0:T(128)}, f32[32,1024]{1,0:T(8,128)}, f32[32,1024]{1,0:T(8,128)}) custom-call(bf16[128,512]{1,0:T(8,128)(2,1)} %refs_0_.1, bf16[512,1024]{1,0:T(8,128)(2,1)} %refs_1_.1, f32[1,1024]{1,0:T(1,128)} %bitcast.2, bf16[1024,512]{1,0:T(8,128)(2,1)} %refs_3_.1, bf16[512,1024]{1,0:T(8,128)(2,1)} %refs_4_.1, bf16[1024,512]{1,0:T(8,128)(2,1)} %refs_5_.1, ...), custom_call_target="tpu_custom_call" | custom-call | tf_op jit(solution)/shard_map/pallas_call | solution.py:470
  46.7 1.7 %shard_map.131 = (f32[3]{0:T(128)}, f32[32,1024]{1,0:T(8,128)}, f32[32,1024]{1,0:T(8,128)}) custom-call(f32[3]{0:T(128)} %get-tuple-element.6.err_ref, f32[32,1024]{1,0:T(8,128)} %get-tuple-element.7.up_ref, f32[32,1024]{1,0:T(8,128)} %get-tuple-element.8.down_ref), custom_call_target="tpu_custom_call" | custom-call | tf_op jit(solution)/shard_map/pallas_call | solution.py:481
